TPU v7x, 256 devices: a whole 4x4x8 slice. The times are simulated.
256 devices in a mesh: dp: 32 (over z, x), tensor: 8 (over y, core).
Axes of the slice: x: 4, y: 4, z: 8, core: 2. Of those that a mesh axis runs over, the one named last changes fastest.
Arguments:
- activations: bfloat16 [28672, 4096], P('dp', 'tensor'), may hold values from -6 to 6
- out_grads: bfloat16 [28672, 4096], P('dp', 'tensor'), may hold values from -6 to 6
- gate_act: bfloat16 [28672, 14336], P('dp', 'tensor'), may hold values from -6 to 6
- w_down: bfloat16 [14336, 4096], P('tensor', 'dp'), may hold values from -0.09375 to 0.09375
- proj_in: bfloat16 [4096, 64], P('tensor'), may hold values from -0.09375 to 0.09375
- proj_out: bfloat16 [14336, 64], P('tensor'), may hold values from -0.046875 to 0.046875
- lengths: int32 [32, 8], P('dp'), may hold values from 1 to 448, 896 in all within a row
- assign: int32 [256], replicated, may hold values from 0 to 255, each once
Outputs:
- loggrads: float32 [256, 64, 64], P('dp', 'tensor')
Inputs may be any that keep to these rules, and one draw needn't show every extreme that they name: `lengths`: each row gives the token counts of the 8 sequences packed into one data group's 896 rows and sums to 896. `assign`: a permutation of the sequence numbers.
All inputs are finite; a program needn't handle non-finite values.
Results may differ from a plain program's by a relative error of at most 0.013.
Values may be sent and summed in bfloat16 or wider, within the bound.
No kernel may reach another device: no remote copies, remote signals or barrier semaphores. Data moves between devices by JAX's collectives and lax.ppermute only.
A program may use at most 128 MiB of HBM per device.

v0:
```python
import jax
import jax.numpy as jnp
from jax import lax
from jax.sharding import PartitionSpec as P


def shards(activations, out_grads, gate_act, w_down, proj_in, proj_out, lengths, assign):
    tok_rows = activations.shape[0]
    rank_all = proj_in.shape[1]
    full_grads = lax.all_gather(out_grads, "tensor", axis=1, tiled=True)
    hidden_grad = lax.dot_general(
        full_grads,
        lax.all_gather(w_down, "dp", axis=1, tiled=True),
        (((1,), (1,)), ((), ())),
        preferred_element_type=jnp.float32,
    )
    up_grad = (hidden_grad * gate_act.astype(jnp.float32)).astype(jnp.bfloat16)
    out_part = jnp.dot(up_grad, proj_out, preferred_element_type=jnp.float32)
    in_part = jnp.dot(activations, proj_in, preferred_element_type=jnp.float32)
    col_count = rank_all // lax.axis_size("tensor")
    shard_index = lax.axis_index("tensor")
    in_sum, out_sum = lax.psum((in_part, out_part), "tensor")
    in_mine = lax.dynamic_slice_in_dim(in_sum, shard_index * col_count, col_count, 1)
    seq_lengths = lengths[0]
    seq_ends = jnp.cumsum(seq_lengths)
    starts = seq_ends - seq_lengths
    positions = lax.iota(jnp.int32, tok_rows)
    inside = (positions[None, :] >= starts[:, None]) & (positions[None, :] < seq_ends[:, None])
    member = jnp.where(inside, 1.0 / seq_lengths[:, None].astype(jnp.float32), 0.0)
    weighted = member[:, :, None] * in_mine[None, :, :]
    result = jnp.einsum("ctp,tq->cpq", weighted, out_sum, precision=lax.Precision.HIGHEST)
    per_group = seq_lengths.shape[0]
    group_count = lax.axis_size("dp")
    seq_total = per_group * group_count
    group_index = lax.axis_index("dp")
    mine_ids = lax.dynamic_slice_in_dim(assign, group_index * per_group, per_group, 0)
    placing = (mine_ids[None, :] == lax.iota(jnp.int32, seq_total)[:, None]).astype(jnp.float32)
    flat_result = result.reshape(per_group, col_count * rank_all)
    spread = jnp.dot(placing, flat_result, precision=lax.Precision.HIGHEST)
    owned = lax.psum_scatter(
        spread.astype(jnp.bfloat16), "dp", scatter_dimension=0, tiled=True
    ).astype(jnp.float32)
    return owned.reshape(per_group, col_count, rank_all)


def solution(mesh):
    in_specs = (
        P("dp", "tensor"),
        P("dp", "tensor"),
        P("dp", "tensor"),
        P("tensor", "dp"),
        P("tensor", None),
        P("tensor", None),
        P("dp", None),
        P(),
    )
    out_specs = P("dp", "tensor", None)
    return jax.shard_map(shards, mesh=mesh, in_specs=in_specs, out_specs=out_specs, check_vma=False)
```

profile of v0, /device:TPU:8, one launch (start us, length us, event | category | flops | bytes accessed | tf_op | source)
XLA Modules:
  0.0 511.5 jit_solution(17634856475808253684)
XLA Ops:
  6.5 0.0 copy-start
  6.5 0.0 all-gather.3.cloned.1.call-start
  6.5 0.7 all-gather.3.cloned.1.call-update
  7.3 0.0 all-gather.5.cloned.1.call-start
  7.3 0.7 all-gather.5.cloned.1.call-update
  8.0 0.0 all-reduce.3.cloned.1.call-start
  8.1 0.8 reduce-window.7
  8.9 0.7 bitcast_subtract_fusion
  9.5 0.0 copy-done
  9.5 2.0 fusion.10
  11.5 0.0 copy-start.2
  11.5 0.0 copy-start.1
  11.5 47.6 %all-gather.3.cloned.1.call-done = bf16[896,4096]{1,0:T(8,128)(2,1)} async-done(((bf16[896,512]{1,0:T(8,128)(2,1)}), bf16[896,4096]{1,0:T(8,128)(2,1)}) %all-gather.3.cloned.1.call-update) | async-done | bytes 7340048 | tf_op jit(solution)/shard_map/all_gather | solution.py:10
  59.1 142.3 %all-gather.5.cloned.1.call-done = bf16[1792,4096]{1,0:T(8,128)(2,1)} async-done(((bf16[1792,128]{1,0:T(8,128)(2,1)}), bf16[1792,4096]{1,0:T(8,128)(2,1)}) %all-gather.5.cloned.1.call-update) | async-done | bytes 14680080 | tf_op jit(solution)/shard_map/all_gather | solution.py:13
  201.4 23.2 %fusion = f32[896,64]{0,1:T(8,128)} fusion(bf16[1792,64]{0,1:T(8,128)(2,1)} %param.13, bf16[896,1792]{1,0:T(8,128)(2,1)} %param.10, bf16[896,4096]{1,0:T(8,128)(2,1)} %all-gather.3.cloned.1.call-done, bf16[1792,4096]{1,0:T(8,128)(2,1)} %all-gather.5.cloned.1.call-done), kind=kOutput, calls=%fused_computation.1 | convolution fusion | flops 13363675136 | bytes 25690112 | tf_op jit(solution)/shard_map/dot_general | solution.py:18
  224.6 0.0 all-reduce.3.cloned.1.call-update
  224.7 0.0 reduce-scatter.2.cloned.1.call-start
  224.7 0.0 copy-done.2
  224.7 0.0 copy-done.1
  224.8 0.1 dynamic_slice.6
  224.8 0.1 fusion.8
  224.9 60.4 %all-reduce.3.cloned.1.call-done = (f32[896,64]{0,1:T(8,128)}, f32[896,64]{0,1:T(8,128)}) async-done(((f32[896,64]{0,1:T(8,128)}, f32[896,64]{0,1:T(8,128)}), (f32[896,64]{0,1:T(8,128)}, f32[896,64]{0,1:T(8,128)})) %all-reduce.3.cloned.1.call-update) | async-done | bytes 458768 | tf_op jit(solution)/shard_map/psum | solution.py:22
  285.3 0.8 constant_dynamic-slice_fusion
  286.1 1.3 fusion.1
  287.4 0.1 reshape.108
  287.5 1.0 convolution_convert_fusion
  288.5 0.0 reduce-scatter.2.cloned.1.call-update
  288.5 215.0 %reduce-scatter.2.cloned.1.call-done = bf16[8,512]{1,0:T(8,128)(2,1)} async-done(((bf16[256,512]{1,0:T(8,128)(2,1)}), bf16[8,512]{1,0:T(8,128)(2,1)}) %reduce-scatter.2.cloned.1.call-update) | async-done | bytes 8208 | tf_op jit(solution)/shard_map/reduce_scatter | solution.py:40
  503.6 1.4 reshape.112
  (1 shorter events, 0.0 us)
Async XLA Ops:
  6.5 3.0 copy-start
  6.5 52.6 %all-gather.3.cloned.1.call-start = ((), (), s32[]{:S(2)}) async-start(), calls=%async_computation.1 | async-start | bytes 8257536 | tf_op jit(solution)/shard_map/all_gather | solution.py:10
  7.3 194.2 %all-gather.5.cloned.1.call-start = ((), (), s32[]{:S(2)}) async-start(), calls=%async_computation.2 | async-start | bytes 15138816 | tf_op jit(solution)/shard_map/all_gather | solution.py:13
  8.0 277.3 %all-reduce.3.cloned.1.call-start = ((), (), s32[]{:S(2)}) async-start(), calls=%async_computation.4 | async-start | bytes 917504 | tf_op jit(solution)/shard_map/psum | solution.py:22
  11.5 213.2 %copy-start.2 = (s32[1,8]{1,0:T(1,128)S(1)}, s32[1,8]{1,0:T(1,128)}, u32[]{:S(2)}) copy-start(s32[1,8]{1,0:T(1,128)} %param.14) | copy-start | bytes 100
  11.5 213.2 %copy-start.1 = (s32[256]{0:T(256)S(1)}, s32[256]{0:T(256)}, u32[]{:S(2)}) copy-start(s32[256]{0:T(256)} %param.15) | copy-start | bytes 3076
  224.7 278.9 %reduce-scatter.2.cloned.1.call-start = ((), (), s32[]{:S(2)}) async-start(), calls=%async_computation.3 | async-start | bytes 270336 | tf_op jit(solution)/shard_map/reduce_scatter | solution.py:40
Sparse Core Ops, SparseCore 0:
  9.2 49.8 all-gather.2
  61.6 139.7 all-gather.4
  224.8 60.4 all-reduce.2
  289.5 214.0 reduce-scatter.1
where the time goes:
time: 512 us; the launch traced here: 511 us
  waiting for transfers between devices  467 us (91%)
  matrix products  27.5 us (5%)
  between operations  13.2 us (3%)
    reduce_scatter x1, waiting for transfers between devices, shards(): lax.psum_scatter(spread.astype(jnp.bfloat16), 'dp', scatter_dimension=0,...  215 us
    all_gather x1, waiting for transfers between devices, shards(): lax.all_gather(w_down, 'dp', axis=1, tiled=True)  142 us
    psum x1, waiting for transfers between devices, shards(): in_sum, out_sum = lax.psum((in_part, out_part), 'tensor')  60.4 us
    all_gather x1, waiting for transfers between devices, shards(): full_grads = lax.all_gather(out_grads, 'tensor', axis=1, tiled=True)  47.6 us
    dot_general x1, matrix products, shards(): out_part = jnp.dot(up_grad, proj_out, preferred_element_type=jnp.float32)  23.2 us
  transfers between devices with their start and end apart: 4, of which 4 were waited for; matrix products, arithmetic and copies ran while one was open for 1% of the time, Pallas kernels for 0%

commit v1 on v0

--- a/solution.py
+++ b/solution.py
@@ -7,7 +7,14 @@
 def shards(activations, out_grads, gate_act, w_down, proj_in, proj_out, lengths, assign):
     tok_rows = activations.shape[0]
     rank_all = proj_in.shape[1]
-    full_grads = lax.all_gather(out_grads, "tensor", axis=1, tiled=True)
+    ring = [out_grads]
+    for hop in range(7):
+        ring.append(lax.ppermute(ring[-1], "tensor", [(dev, (dev + 1) % 8) for dev in range(8)]))
+    full_grads = jnp.roll(
+        jnp.concatenate(ring[::-1], axis=1),
+        (lax.axis_index("tensor") + 1) * ring[0].shape[1],
+        axis=1,
+    )
     hidden_grad = lax.dot_general(
         full_grads,
         lax.all_gather(w_down, "dp", axis=1, tiled=True),

time: 512 us -> 462 us (0.902)
  waiting for transfers between devices: 467 us -> 386 us
  local copies, waits for them, and re-layouts: 2.3 us -> 32.4 us
    all_gather x1, waiting for transfers between devices: 142 us -> 23.6 us  [shards(): lax.all_gather(w_down, 'dp', axis=1, tiled=True)]
    ppermute x0 -> x7, waiting for transfers between devices: none -> 86.4 us  [shards(): lax.ppermute(ring[-1], 'tensor', [(dev, (dev + 1) % 8) for dev in range(8)])]
    all_gather x1 -> x0, waiting for transfers between devices: 47.6 us -> none  [shards(): full_grads = lax.all_gather(out_grads, 'tensor', axis=1, tiled=True)]
    unnamed x6 -> x41, local copies, waits for them, and re-layouts: 0.01 us -> 29 us
  transfers between devices with their start and end apart: 4 -> 10, of which waited for: 4 -> 10; matrix products, arithmetic and copies ran while one was open for 1% -> 7% of each run, Pallas kernels for 0% -> 0%
where the time goes in v1:
time: 462 us; the launch traced here: 461 us
  waiting for transfers between devices  386 us (84%)
  local copies, waits for them, and re-layouts  32.4 us (7%)
  matrix products  27.3 us (6%)
  between operations  13.2 us (3%)
    reduce_scatter x1, waiting for transfers between devices, shards(): lax.psum_scatter(spread.astype(jnp.bfloat16), 'dp', scatter_dimension=0,...  215 us
    ppermute x7, waiting for transfers between devices, shards(): lax.ppermute(ring[-1], 'tensor', [(dev, (dev + 1) % 8) for dev in range(8)])  86.4 us
    psum x1, waiting for transfers between devices, shards(): in_sum, out_sum = lax.psum((in_part, out_part), 'tensor')  60.5 us
    unnamed x41, local copies, waits for them, and re-layouts  29 us
    all_gather x1, waiting for transfers between devices, shards(): lax.all_gather(w_down, 'dp', axis=1, tiled=True)  23.6 us
    dot_general x1, matrix products, shards(): out_part = jnp.dot(up_grad, proj_out, preferred_element_type=jnp.float32)  22.7 us
  transfers between devices with their start and end apart: 10, of which 10 were waited for; matrix products, arithmetic and copies ran while one was open for 7% of the time, Pallas kernels for 0%

profile of v1, /device:TPU:8, one launch (start us, length us, event | category | flops | bytes accessed | tf_op | source)
XLA Modules:
  0.0 461.1 jit_solution(4586262221011154526)
XLA Ops:
  6.5 0.0 copy-start
  6.5 0.0 all-gather.2.cloned.1.call-start
  6.5 0.7 all-gather.2.cloned.1.call-update
  7.3 0.0 all-reduce.3.cloned.1.call-start
  7.3 0.0 collective-permute-start
  7.3 13.0 %collective-permute-done = bf16[896,512]{1,0:T(8,128)(2,1)S(1)} collective-permute-done((bf16[896,512]{1,0:T(8,128)(2,1)}, bf16[896,512]{1,0:T(8,128)(2,1)S(1)}, u32[]{:S(2)}, u32[]{:S(2)}) %collective-permute-start) | collective-permute-done | bytes 917536 | tf_op jit(solution)/shard_map/ppermute | solution.py:12
  20.3 0.0 collective-permute-start.1
  20.4 12.8 %collective-permute-done.1 = bf16[896,512]{1,0:T(8,128)(2,1)S(1)} collective-permute-done((bf16[896,512]{1,0:T(8,128)(2,1)S(1)}, bf16[896,512]{1,0:T(8,128)(2,1)S(1)}, u32[]{:S(2)}, u32[]{:S(2)}) %collective-permute-start.1) | collective-permute-done | bytes 917536 | tf_op jit(solution)/shard_map/ppermute | solution.py:12
  33.2 1.0 copy-done.2
  34.2 0.0 collective-permute-start.2
  34.2 12.8 %collective-permute-done.2 = bf16[896,512]{1,0:T(8,128)(2,1)S(1)} collective-permute-done((bf16[896,512]{1,0:T(8,128)(2,1)S(1)}, bf16[896,512]{1,0:T(8,128)(2,1)S(1)}, u32[]{:S(2)}, u32[]{:S(2)}) %collective-permute-start.2) | collective-permute-done | bytes 917536 | tf_op jit(solution)/shard_map/ppermute | solution.py:12
  47.0 0.9 copy-done.4
  47.9 0.0 collective-permute-start.3
  47.9 12.8 %collective-permute-done.3 = bf16[896,512]{1,0:T(8,128)(2,1)S(1)} collective-permute-done((bf16[896,512]{1,0:T(8,128)(2,1)S(1)}, bf16[896,512]{1,0:T(8,128)(2,1)S(1)}, u32[]{:S(2)}, u32[]{:S(2)}) %collective-permute-start.3) | collective-permute-done | bytes 917536 | tf_op jit(solution)/shard_map/ppermute | solution.py:12
  60.7 0.9 copy-done.6
  61.7 0.0 collective-permute-start.4
  61.7 12.8 %collective-permute-done.4 = bf16[896,512]{1,0:T(8,128)(2,1)S(1)} collective-permute-done((bf16[896,512]{1,0:T(8,128)(2,1)S(1)}, bf16[896,512]{1,0:T(8,128)(2,1)S(1)}, u32[]{:S(2)}, u32[]{:S(2)}) %collective-permute-start.4) | collective-permute-done | bytes 917536 | tf_op jit(solution)/shard_map/ppermute | solution.py:12
  74.5 0.9 copy-done.8
  75.4 0.0 collective-permute-start.5
  75.4 12.9 %collective-permute-done.5 = bf16[896,512]{1,0:T(8,128)(2,1)} collective-permute-done((bf16[896,512]{1,0:T(8,128)(2,1)S(1)}, bf16[896,512]{1,0:T(8,128)(2,1)}, u32[]{:S(2)}, u32[]{:S(2)}) %collective-permute-start.5) | collective-permute-done | bytes 917536 | tf_op jit(solution)/shard_map/ppermute | solution.py:12
  88.4 0.0 collective-permute-start.6
  88.4 0.8 reduce-window.7
  89.2 0.8 bitcast_subtract_fusion
  90.0 0.0 copy-done
  90.0 2.2 fusion.18
  92.3 9.2 %collective-permute-done.6 = bf16[896,512]{1,0:T(8,128)(2,1)} collective-permute-done((bf16[896,512]{1,0:T(8,128)(2,1)}, bf16[896,512]{1,0:T(8,128)(2,1)}, u32[]{:S(2)}, u32[]{:S(2)}) %collective-permute-start.6) | collective-permute-done | bytes 917536 | tf_op jit(solution)/shard_map/ppermute | solution.py:12
  101.5 2.3 constant_dynamic-update-slice_fusion.15
  103.8 2.2 constant_dynamic-update-slice_fusion.14
  106.0 2.2 constant_dynamic-update-slice_fusion.13
  108.2 2.3 constant_dynamic-update-slice_fusion.12
  110.5 2.2 constant_dynamic-update-slice_fusion.11
  112.7 2.2 constant_dynamic-update-slice_fusion.10
  115.0 1.0 constant_dynamic-update-slice_fusion.9
  116.0 0.0 copy-done.1
  116.0 1.1 constant_dynamic-update-slice_fusion.8
  117.1 2.2 constant_dynamic-update-slice_fusion.7
  119.3 2.3 constant_dynamic-update-slice_fusion.6
  121.7 0.0 copy-done.9
  121.7 1.0 constant_dynamic-update-slice_fusion.5
  122.7 0.0 copy-done.7
  122.7 1.0 constant_dynamic-update-slice_fusion.4
  123.7 0.0 copy-done.5
  123.7 1.0 constant_dynamic-update-slice_fusion.3
  124.7 0.0 copy-done.3
  124.7 1.0 constant_dynamic-update-slice_fusion.2
  125.7 1.0 constant_dynamic-update-slice_fusion.1
  126.7 1.0 constant_dynamic-update-slice_fusion
  127.8 23.6 %all-gather.2.cloned.1.call-done = bf16[1792,4096]{1,0:T(8,128)(2,1)} async-done(((bf16[1792,128]{1,0:T(8,128)(2,1)}), bf16[1792,4096]{1,0:T(8,128)(2,1)}) %all-gather.2.cloned.1.call-update) | async-done | bytes 14680080 | tf_op jit(solution)/shard_map/all_gather | solution.py:20
  151.4 0.0 copy-done.10
  151.4 22.7 %fusion.5 = f32[896,64]{0,1:T(8,128)} fusion(bf16[1792,64]{0,1:T(8,128)(2,1)S(1)} %copy-done.10, bf16[896,1792]{1,0:T(8,128)(2,1)} %param.10, bf16[1792,4096]{1,0:T(8,128)(2,1)} %all-gather.2.cloned.1.call-done, bf16[896,8192]{1,0:T(8,128)(2,1)} %constant_dynamic-update-slice_fusion, s32[]{:T(128)S(6)} %select_n.31), kind=kOutput, calls=%fused_computation.3 | convolution fusion | flops 13363675136 | bytes 25690116 | tf_op jit(solution)/shard_map/dot_general | solution.py:25
  174.1 0.0 all-reduce.3.cloned.1.call-update
  174.1 0.0 reduce-scatter.2.cloned.1.call-start
  174.2 0.0 copy-done.12
  174.2 0.0 copy-done.11
  174.2 0.1 dynamic_slice.10
  174.3 0.1 fusion.14
  174.3 60.5 %all-reduce.3.cloned.1.call-done = (f32[896,64]{0,1:T(8,128)}, f32[896,64]{0,1:T(8,128)}) async-done(((f32[896,64]{0,1:T(8,128)}, f32[896,64]{0,1:T(8,128)}), (f32[896,64]{0,1:T(8,128)}, f32[896,64]{0,1:T(8,128)})) %all-reduce.3.cloned.1.call-update) | async-done | bytes 458768 | tf_op jit(solution)/shard_map/psum | solution.py:29
  234.9 0.8 constant_dynamic-slice_fusion
  235.6 1.3 fusion.7
  236.9 0.1 reshape.108
  237.0 1.0 convolution_convert_fusion
  238.0 0.0 reduce-scatter.2.cloned.1.call-update
  238.1 215.1 %reduce-scatter.2.cloned.1.call-done = bf16[8,512]{1,0:T(8,128)(2,1)} async-done(((bf16[256,512]{1,0:T(8,128)(2,1)}), bf16[8,512]{1,0:T(8,128)(2,1)}) %reduce-scatter.2.cloned.1.call-update) | async-done | bytes 8208 | tf_op jit(solution)/shard_map/reduce_scatter | solution.py:47
  453.2 1.4 reshape.112
  (13 shorter events, 0.0 us)
Async XLA Ops:
  6.5 83.5 %copy-start = (bf16[896,512]{1,0:T(8,128)(2,1)S(1)}, bf16[896,512]{1,0:T(8,128)(2,1)}, u32[]{:S(2)}) copy-start(bf16[896,512]{1,0:T(8,128)(2,1)} %param.8) | copy-start | bytes 2752516
  6.5 109.5 %copy-start.1 = (bf16[896,512]{1,0:T(8,128)(2,1)S(1)}, bf16[896,512]{1,0:T(8,128)(2,1)}, u32[]{:S(2)}) copy-start(bf16[896,512]{1,0:T(8,128)(2,1)} %param.9) | copy-start | bytes 2752516
  6.5 144.8 %all-gather.2.cloned.1.call-start = ((), (), s32[]{:S(2)}) async-start(), calls=%async_computation.1 | async-start | bytes 15138816 | tf_op jit(solution)/shard_map/all_gather | solution.py:20
  7.3 227.6 %all-reduce.3.cloned.1.call-start = ((), (), s32[]{:S(2)}) async-start(), calls=%async_computation.3 | async-start | bytes 917504 | tf_op jit(solution)/shard_map/psum | solution.py:29
  7.3 13.0 %collective-permute-start = (bf16[896,512]{1,0:T(8,128)(2,1)}, bf16[896,512]{1,0:T(8,128)(2,1)S(1)}, u32[]{:S(2)}, u32[]{:S(2)}) collective-permute-start(bf16[896,512]{1,0:T(8,128)(2,1)} %param.9), channel_id=1, source_target_pairs={{0,1},{1,2},{2,3},{3,4},{4,5},{5,6},{6,7},{7,0},{8,9},{9,10},{10,1... | collective-permute-start | bytes 2752520 | tf_op jit(solution)/shard_map/ppermute | solution.py:12
  20.3 12.8 %collective-permute-start.1 = (bf16[896,512]{1,0:T(8,128)(2,1)S(1)}, bf16[896,512]{1,0:T(8,128)(2,1)S(1)}, u32[]{:S(2)}, u32[]{:S(2)}) collective-permute-start(bf16[896,512]{1,0:T(8,128)(2,1)S(1)} %collective-permute-done), channel_id=1, source_target_pairs={{0,1},{1,2},{2,3},{3,4},{4,5},{5,6},{6,7},{7,0},{8,9},{9,10},{10,1... | collective-permute-start | bytes 2752520 | tf_op jit(solution)/shard_map/ppermute | solution.py:12
  33.2 1.0 copy-start.2
  34.2 12.8 %collective-permute-start.2 = (bf16[896,512]{1,0:T(8,128)(2,1)S(1)}, bf16[896,512]{1,0:T(8,128)(2,1)S(1)}, u32[]{:S(2)}, u32[]{:S(2)}) collective-permute-start(bf16[896,512]{1,0:T(8,128)(2,1)S(1)} %collective-permute-done.1), channel_id=1, source_target_pairs={{0,1},{1,2},{2,3},{3,4},{4,5},{5,6},{6,7},{7,0},{8,9},{9,10},{10,1... | collective-permute-start | bytes 2752520 | tf_op jit(solution)/shard_map/ppermute | solution.py:12
  47.0 0.9 copy-start.4
  47.9 12.8 %collective-permute-start.3 = (bf16[896,512]{1,0:T(8,128)(2,1)S(1)}, bf16[896,512]{1,0:T(8,128)(2,1)S(1)}, u32[]{:S(2)}, u32[]{:S(2)}) collective-permute-start(bf16[896,512]{1,0:T(8,128)(2,1)S(1)} %collective-permute-done.2), channel_id=1, source_target_pairs={{0,1},{1,2},{2,3},{3,4},{4,5},{5,6},{6,7},{7,0},{8,9},{9,10},{10,1... | collective-permute-start | bytes 2752520 | tf_op jit(solution)/shard_map/ppermute | solution.py:12
  60.7 0.9 copy-start.6
  61.7 12.8 %collective-permute-start.4 = (bf16[896,512]{1,0:T(8,128)(2,1)S(1)}, bf16[896,512]{1,0:T(8,128)(2,1)S(1)}, u32[]{:S(2)}, u32[]{:S(2)}) collective-permute-start(bf16[896,512]{1,0:T(8,128)(2,1)S(1)} %collective-permute-done.3), channel_id=1, source_target_pairs={{0,1},{1,2},{2,3},{3,4},{4,5},{5,6},{6,7},{7,0},{8,9},{9,10},{10,1... | collective-permute-start | bytes 2752520 | tf_op jit(solution)/shard_map/ppermute | solution.py:12
  74.5 0.9 copy-start.8
  75.4 12.9 %collective-permute-start.5 = (bf16[896,512]{1,0:T(8,128)(2,1)S(1)}, bf16[896,512]{1,0:T(8,128)(2,1)}, u32[]{:S(2)}, u32[]{:S(2)}) collective-permute-start(bf16[896,512]{1,0:T(8,128)(2,1)S(1)} %collective-permute-done.4), channel_id=1, source_target_pairs={{0,1},{1,2},{2,3},{3,4},{4,5},{5,6},{6,7},{7,0},{8,9},{9,10},{10,1... | collective-permute-start | bytes 2752520 | tf_op jit(solution)/shard_map/ppermute | solution.py:12
  88.4 13.1 %collective-permute-start.6 = (bf16[896,512]{1,0:T(8,128)(2,1)}, bf16[896,512]{1,0:T(8,128)(2,1)}, u32[]{:S(2)}, u32[]{:S(2)}) collective-permute-start(bf16[896,512]{1,0:T(8,128)(2,1)} %collective-permute-done.5), channel_id=1, source_target_pairs={{0,1},{1,2},{2,3},{3,4},{4,5},{5,6},{6,7},{7,0},{8,9},{9,10},{10,1... | collective-permute-start | bytes 2752520 | tf_op jit(solution)/shard_map/ppermute | solution.py:12
  89.2 32.4 %copy-start.9 = (bf16[896,512]{1,0:T(8,128)(2,1)S(1)}, bf16[896,512]{1,0:T(8,128)(2,1)}, u32[]{:S(2)}) copy-start(bf16[896,512]{1,0:T(8,128)(2,1)} %copy-done.8) | copy-start | bytes 2752516
  89.2 33.5 %copy-start.7 = (bf16[896,512]{1,0:T(8,128)(2,1)S(1)}, bf16[896,512]{1,0:T(8,128)(2,1)}, u32[]{:S(2)}) copy-start(bf16[896,512]{1,0:T(8,128)(2,1)} %copy-done.6) | copy-start | bytes 2752516
  89.2 34.5 %copy-start.5 = (bf16[896,512]{1,0:T(8,128)(2,1)S(1)}, bf16[896,512]{1,0:T(8,128)(2,1)}, u32[]{:S(2)}) copy-start(bf16[896,512]{1,0:T(8,128)(2,1)} %copy-done.4) | copy-start | bytes 2752516
  89.2 35.5 %copy-start.3 = (bf16[896,512]{1,0:T(8,128)(2,1)S(1)}, bf16[896,512]{1,0:T(8,128)(2,1)}, u32[]{:S(2)}) copy-start(bf16[896,512]{1,0:T(8,128)(2,1)} %copy-done.2) | copy-start | bytes 2752516
  92.3 59.1 %copy-start.10 = (bf16[1792,64]{0,1:T(8,128)(2,1)S(1)}, bf16[1792,64]{0,1:T(8,128)(2,1)}, u32[]{:S(2)}) copy-start(bf16[1792,64]{0,1:T(8,128)(2,1)} %param.13) | copy-start | bytes 688132
  127.8 46.4 %copy-start.12 = (s32[1,8]{1,0:T(1,128)S(1)}, s32[1,8]{1,0:T(1,128)}, u32[]{:S(2)}) copy-start(s32[1,8]{1,0:T(1,128)} %param.14) | copy-start | bytes 100
  127.8 46.4 %copy-start.11 = (s32[256]{0:T(256)S(1)}, s32[256]{0:T(256)}, u32[]{:S(2)}) copy-start(s32[256]{0:T(256)} %param.15) | copy-start | bytes 3076
  174.1 279.1 %reduce-scatter.2.cloned.1.call-start = ((), (), s32[]{:S(2)}) async-start(), calls=%async_computation.2 | async-start | bytes 270336 | tf_op jit(solution)/shard_map/reduce_scatter | solution.py:47
Sparse Core Ops, SparseCore 0:
  9.8 141.4 all-gather.1
  174.2 60.5 all-reduce.2
  239.2 213.9 reduce-scatter.1
